TPU v7x, 32 devices: a whole 2x2x4 slice. The times are simulated.
32 devices in a mesh: seq: 16 (over z, x, core), head: 2 (over y).
Axes of the slice: x: 2, y: 2, z: 4, core: 2. Of those that a mesh axis runs over, the one named last changes fastest.
Arguments:
- activations: bfloat16 [2048, 2048], P('seq'), may hold values from -6 to 6
- doc_ids: int32 [2048], replicated, may hold values from 0 to 1, as said below
- w_query: bfloat16 [2048, 2048], P(None, 'head'), may hold values from -0.125 to 0.125
- w_key: bfloat16 [2048, 2048], P(None, 'head'), may hold values from -0.125 to 0.125
- w_value: bfloat16 [2048, 2048], P(None, 'head'), may hold values from -0.125 to 0.125
- w_out: bfloat16 [2048, 2048], P('head'), may hold values from -1.5 to 1.5
- w_gate: bfloat16 [2048, 8192], P(None, 'head'), may hold values from -0.125 to 0.125
- w_up: bfloat16 [2048, 8192], P(None, 'head'), may hold values from -0.125 to 0.125
- w_down: bfloat16 [8192, 2048], P('head'), may hold values from -0.0625 to 0.0625
- gain_attn: float32 [2048], replicated, may hold values from 0.5 to 1.5
- gain_mlp: float32 [2048], replicated, may hold values from 0.5 to 1.5
- cotangent: bfloat16 [2048, 2048], P('seq'), may hold values from -6 to 6
Outputs:
- output: bfloat16 [2048, 2048], P('seq')
- input_grad: bfloat16 [2048, 2048], P('seq')
- query_grad: float32 [2048, 2048], P('seq', 'head')
- key_grad: float32 [2048, 2048], P('seq', 'head')
- value_grad: float32 [2048, 2048], P('seq', 'head')
- out_grad: float32 [2048, 2048], P('head', 'seq')
- gate_grad: float32 [2048, 8192], P('seq', 'head')
- up_grad: float32 [2048, 8192], P('seq', 'head')
- down_grad: float32 [8192, 2048], P('head', 'seq')
- gain_attn_grad: float32 [2048], P('seq')
- gain_mlp_grad: float32 [2048], P('seq')
Inputs may be any that keep to these rules, and one draw needn't show every extreme that they name: `doc_ids`: document number of each token, never falling along the tokens; each document is one packed sequence of about 2048 / 2 tokens.
All inputs are finite; a program needn't handle non-finite values.
Results may differ from a plain program's by a relative error of at most 0.014.
Values may be sent and summed in bfloat16 or wider, within the bound.
No kernel may reach another device: no remote copies, remote signals or barrier semaphores. Data moves between devices by JAX's collectives and lax.ppermute only.
A program may use at most 320 MiB of HBM per device.

v0:
```python
import math

import jax
import jax.numpy as jnp
from jax import lax
from jax.sharding import PartitionSpec as P

HD = 128
BIAS_LEN = 4096


def frequencies(head_dim):
    half_dim = head_dim // 2
    return jnp.exp(-jnp.arange(half_dim).astype(jnp.float32) * (2.0 / head_dim) * math.log(10000.0))


def turned(values, angles):
    half_dim = values.shape[-1] // 2
    cosine = jnp.cos(angles)[:, None, :]
    sine = jnp.sin(angles)[:, None, :]
    former = values[..., :half_dim]
    latter = values[..., half_dim:]
    return jnp.concatenate(
        [former * cosine - latter * sine, former * sine + latter * cosine], axis=-1
    )


def normalized(values, gain):
    inverse = lax.rsqrt(jnp.mean(values * values, axis=-1, keepdims=True) + 1e-05)
    return (values * inverse * gain, inverse)


def norm_back(values, inverse, gain, upstream):
    scaled = values * inverse
    gain_term = jnp.sum(upstream * scaled, axis=0)
    weighted = upstream * gain
    return (
        inverse * (weighted - scaled * jnp.mean(weighted * scaled, axis=-1, keepdims=True)),
        gain_term,
    )


def project(factor_one, factor_two):
    return jnp.dot(factor_one, factor_two, preferred_element_type=jnp.float32)


def contract_rows(factor_one, factor_two):
    return lax.dot_general(
        factor_one, factor_two, (((0,), (0,)), ((), ())), preferred_element_type=jnp.float32
    )


def project_back(factor_one, factor_two):
    return lax.dot_general(
        factor_one, factor_two, (((1,), (1,)), ((), ())), preferred_element_type=jnp.float32
    )


def key_mask(query_docs, query_places, key_start, key_count, doc_ids):
    key_docs = lax.dynamic_slice_in_dim(doc_ids, key_start, key_count, 0)
    key_places = key_start + jnp.arange(key_count, dtype=jnp.int32)
    return (query_docs[:, None] == key_docs[None, :]) & (
        key_places[None, :] <= query_places[:, None]
    )


def sigmoid_weights(query_block, key_block, allowed):
    scores = jnp.einsum(
        "qhd,khd->hqk", query_block, key_block, preferred_element_type=jnp.float32
    ) * HD ** (-0.5) - math.log(BIAS_LEN)
    return jnp.where(allowed[None], jax.nn.sigmoid(scores), 0.0)


def local(
    activations,
    doc_ids,
    w_query,
    w_key,
    w_value,
    w_out,
    w_gate,
    w_up,
    w_down,
    gain_attn,
    gain_mlp,
    cotangent,
):
    local_rows = activations.shape[0]
    total_rows = local_rows * lax.axis_size("seq")
    local_heads = w_query.shape[1] // HD
    local_width = local_heads * HD
    first_row = lax.axis_index("seq") * local_rows
    query_places = first_row + jnp.arange(local_rows, dtype=jnp.int32)
    query_docs = lax.dynamic_slice_in_dim(doc_ids, first_row, local_rows, 0)
    angles = query_places.astype(jnp.float32)[:, None] * frequencies(HD)[None, :]
    score_scale = HD ** (-0.5)
    key_rows = math.gcd(total_rows, 1024)
    key_starts = jnp.arange(total_rows // key_rows, dtype=jnp.int32) * key_rows
    inputs = activations.astype(jnp.float32)
    normed, inverse_attn = normalized(inputs, gain_attn)
    normed_low = normed.astype(jnp.bfloat16)
    query_rot = turned(
        project(normed_low, w_query).reshape(local_rows, local_heads, HD), angles
    ).astype(jnp.bfloat16)
    key_rot = turned(
        project(normed_low, w_key).reshape(local_rows, local_heads, HD), angles
    ).astype(jnp.bfloat16)
    value_rows = (
        project(normed_low, w_value).astype(jnp.bfloat16).reshape(local_rows, local_heads, HD)
    )
    empty_out = jnp.zeros((local_rows, local_heads, HD), jnp.float32)

    def add_keys(carry, pieces, key_start):
        key_block, value_block = pieces
        allowed = key_mask(query_docs, query_places, key_start, key_block.shape[0], doc_ids)
        weights_low = sigmoid_weights(query_rot, key_block, allowed).astype(jnp.bfloat16)
        return carry + jnp.einsum(
            "hqk,khd->qhd", weights_low, value_block, preferred_element_type=jnp.float32
        )

    all_keys, all_values = (
        lax.all_gather(key_rot, "seq", axis=0, tiled=True),
        lax.all_gather(value_rows, "seq", axis=0, tiled=True),
    )

    def forward_block(carry, key_start):
        key_block = lax.dynamic_slice_in_dim(all_keys, key_start, key_rows, 0)
        value_block = lax.dynamic_slice_in_dim(all_values, key_start, key_rows, 0)
        return (add_keys(carry, (key_block, value_block), key_start), None)

    mixed, unused = lax.scan(forward_block, empty_out, key_starts)
    attended = mixed.reshape(local_rows, local_width).astype(jnp.bfloat16)
    branch = lax.psum(project(attended, w_out), "head")
    middle = inputs + branch
    second, inverse_mlp = normalized(middle, gain_mlp)
    second_low = second.astype(jnp.bfloat16)
    gate = project(second_low, w_gate)
    upward = project(second_low, w_up)
    gate_sig = jax.nn.sigmoid(gate)
    hidden_low = (gate * gate_sig * upward).astype(jnp.bfloat16)
    feed = lax.psum(project(hidden_low, w_down), "head")
    output = (middle + feed).astype(jnp.bfloat16)
    grad_out = cotangent.astype(jnp.float32)
    down_term = contract_rows(hidden_low, cotangent)
    hidden_grad = project_back(cotangent, w_down)
    gate_low = (hidden_grad * upward * gate_sig * (1.0 + gate * (1.0 - gate_sig))).astype(
        jnp.bfloat16
    )
    upward_low = (hidden_grad * gate * gate_sig).astype(jnp.bfloat16)
    gate_term = contract_rows(second_low, gate_low)
    upward_term = contract_rows(second_low, upward_low)
    second_part = project_back(gate_low, w_gate) + project_back(upward_low, w_up)
    second_grad = lax.psum(second_part, "head")
    middle_norm_grad, gain_mlp_term = norm_back(middle, inverse_mlp, gain_mlp, second_grad)
    middle_grad = grad_out + middle_norm_grad
    branch_low = middle_grad.astype(jnp.bfloat16)
    out_term = contract_rows(attended, branch_low)
    mixed_grad = (
        project_back(branch_low, w_out).astype(jnp.bfloat16).reshape(local_rows, local_heads, HD)
    )

    def back_block(query_total, key_start):
        key_block = lax.dynamic_slice_in_dim(all_keys, key_start, key_rows, 0)
        value_block = lax.dynamic_slice_in_dim(all_values, key_start, key_rows, 0)
        allowed = key_mask(query_docs, query_places, key_start, key_rows, doc_ids)
        weights_full = sigmoid_weights(query_rot, key_block, allowed)
        weights_low = weights_full.astype(jnp.bfloat16)
        value_part = jnp.einsum(
            "hqk,qhd->khd", weights_low, mixed_grad, preferred_element_type=jnp.float32
        )
        weight_grads = jnp.einsum(
            "qhd,khd->hqk", mixed_grad, value_block, preferred_element_type=jnp.float32
        )
        score_low = (weight_grads * weights_full * (1.0 - weights_full)).astype(jnp.bfloat16)
        query_total = (
            query_total
            + jnp.einsum("hqk,khd->qhd", score_low, key_block, preferred_element_type=jnp.float32)
            * score_scale
        )
        key_part = (
            jnp.einsum("hqk,qhd->khd", score_low, query_rot, preferred_element_type=jnp.float32)
            * score_scale
        )
        return (
            query_total,
            (key_part.reshape(key_rows, local_width), value_part.reshape(key_rows, local_width)),
        )

    query_grad_rot, (key_parts, value_parts) = lax.scan(back_block, empty_out, key_starts)
    key_grad_rot, value_grad = (
        lax.psum_scatter(
            key_parts.reshape(total_rows, local_width), "seq", scatter_dimension=0, tiled=True
        ),
        lax.psum_scatter(
            value_parts.reshape(total_rows, local_width), "seq", scatter_dimension=0, tiled=True
        ),
    )
    query_low = (
        turned(query_grad_rot, -angles).astype(jnp.bfloat16).reshape(local_rows, local_width)
    )
    key_low = (
        turned(key_grad_rot.reshape(local_rows, local_heads, HD), -angles)
        .astype(jnp.bfloat16)
        .reshape(local_rows, local_width)
    )
    value_low = value_grad.astype(jnp.bfloat16)
    query_term = contract_rows(normed_low, query_low)
    key_term = contract_rows(normed_low, key_low)
    value_term = contract_rows(normed_low, value_low)
    normed_part = (
        project_back(query_low, w_query)
        + project_back(key_low, w_key)
        + project_back(value_low, w_value)
    )
    normed_grad = lax.psum(normed_part, "head")
    input_norm_grad, gain_attn_term = norm_back(inputs, inverse_attn, gain_attn, normed_grad)
    input_grad = (middle_grad + input_norm_grad).astype(jnp.bfloat16)
    (
        query_sum,
        key_sum,
        value_sum,
        out_sum,
        gate_sum,
        up_sum,
        down_sum,
        gain_attn_sum,
        gain_mlp_sum,
    ) = (
        lax.psum_scatter(query_term, "seq", scatter_dimension=0, tiled=True),
        lax.psum_scatter(key_term, "seq", scatter_dimension=0, tiled=True),
        lax.psum_scatter(value_term, "seq", scatter_dimension=0, tiled=True),
        lax.psum_scatter(out_term, "seq", scatter_dimension=1, tiled=True),
        lax.psum_scatter(gate_term, "seq", scatter_dimension=0, tiled=True),
        lax.psum_scatter(upward_term, "seq", scatter_dimension=0, tiled=True),
        lax.psum_scatter(down_term, "seq", scatter_dimension=1, tiled=True),
        lax.psum_scatter(gain_attn_term, "seq", scatter_dimension=0, tiled=True),
        lax.psum_scatter(gain_mlp_term, "seq", scatter_dimension=0, tiled=True),
    )
    return (
        output,
        input_grad,
        query_sum,
        key_sum,
        value_sum,
        out_sum,
        gate_sum,
        up_sum,
        down_sum,
        gain_attn_sum,
        gain_mlp_sum,
    )


def solution(mesh):
    placed = (
        P("seq", None),
        P(),
        P(None, "head"),
        P(None, "head"),
        P(None, "head"),
        P("head", None),
        P(None, "head"),
        P(None, "head"),
        P("head", None),
        P(),
        P(),
        P("seq", None),
    )
    return jax.shard_map(
        local,
        mesh=mesh,
        in_specs=placed,
        out_specs=(
            P("seq", None),
            P("seq", None),
            P("seq", "head"),
            P("seq", "head"),
            P("seq", "head"),
            P("head", "seq"),
            P("seq", "head"),
            P("seq", "head"),
            P("head", "seq"),
            P("seq"),
            P("seq"),
        ),
        check_vma=False,
    )
```

profile of v0, /device:TPU:0, one launch (start us, length us, event | category | flops | bytes accessed | tf_op | source)
XLA Modules:
  0.0 2124.7 jit_solution(2151360301415900347)
XLA Ops:
  7.3 1.3 fusion.54
  8.6 4.3 fusion.68
  12.9 1.8 fusion.70
  16.6 3.0 fusion.46
  20.8 51.9 %all-gather.5.cloned.1.call-done = bf16[2048,8,128]{0,2,1:T(8,128)(2,1)} async-done(((bf16[128,8,128]{0,2,1:T(8,128)(2,1)}), bf16[2048,8,128]{0,2,1:T(8,128)(2,1)}) %all-gather.5.cloned.1.call-update) | async-done | bytes 4194320 | tf_op jit(solution)/shard_map/all_gather | solution.py:122
  72.7 6.5 copy.99
  79.1 45.1 %all-gather.3.cloned.1.call-done = bf16[2048,8,128]{2,0,1:T(8,128)(2,1)} async-done(((bf16[128,8,128]{2,0,1:T(8,128)(2,1)}), bf16[2048,8,128]{2,0,1:T(8,128)(2,1)}) %all-gather.3.cloned.1.call-update) | async-done | bytes 4194320 | tf_op jit(solution)/shard_map/all_gather | solution.py:123
  124.2 16.9 while.30
  127.8 4.8 fusion.141
  136.3 4.8 fusion.141
  141.2 4.0 fusion.73
  145.5 38.4 %all-reduce.8.cloned.1.call-done = f32[128,2048]{1,0:T(8,128)} async-done(((f32[128,2048]{1,0:T(8,128)}), f32[128,2048]{1,0:T(8,128)}) %all-reduce.8.cloned.1.call-update) | async-done | bytes 1048592 | tf_op jit(solution)/shard_map/psum | solution.py:133
  183.9 1.4 multiply_reduce_fusion.2
  185.6 9.8 fusion.74
  195.4 9.5 fusion.75
  204.9 14.4 multiply_convert_fusion
  219.3 23.5 %fusion.77 = f32[128,2048]{1,0:T(8,128)} fusion(bf16[128,4096]{1,0:T(8,128)(2,1)} %get-tuple-element.493, bf16[2048,4096]{1,0:T(8,128)(2,1)} %param.22), kind=kOutput, calls=%fused_computation.109 | convolution fusion | flops 2147483648 | bytes 18874368 | tf_op jit(solution)/shard_map/dot_general | solution.py:54
  242.8 12.6 convolution_add_fusion.2
  255.5 40.1 %all-reduce.10.cloned.1.call-done = f32[128,2048]{1,0:T(8,128)} async-done(((f32[128,2048]{1,0:T(8,128)}), f32[128,2048]{1,0:T(8,128)}) %all-reduce.10.cloned.1.call-update) | async-done | bytes 1048592 | tf_op jit(solution)/shard_map/psum | solution.py:153
  295.6 2.3 multiply_reduce_fusion
  297.9 1.5 multiply_add_fusion
  300.5 1.5 convolution_convert_fusion
  302.2 83.4 %while.31 = (s32[]{:T(128)}, f32[128,8,128]{0,2,1:T(8,128)S(1)}, f32[2,1024,1024]{2,1,0:T(8,128)}, f32[2,1024,1024]{2,1,0:T(8,128)}, s32[2]{0:T(128)S(1)}, /*ind...) while((s32[]{:T(128)}, f32[128,8,128]{0,2,1:T(8,128)S(1)}, ...), condition=%wide.region_9.10_spmd.clone, body=%wide.region_8.9_spmd.clone.sunk | while | flops 1355547776 | bytes 128210752 | solution.py:189
  305.8 3.4 bitcast_select_fusion.3
  311.2 2.8 fusion.153
  314.0 2.7 fusion.154
  316.7 5.4 copy.136
  322.1 2.7 multiply_bitcast_fusion.2
  324.7 5.4 copy.137
  330.1 5.4 copy.138
  335.5 8.4 constant_dynamic-update-slice_fusion.3
  347.5 3.4 bitcast_select_fusion.3
  352.9 2.8 fusion.153
  355.7 2.7 fusion.154
  358.4 5.4 copy.136
  363.7 2.7 multiply_bitcast_fusion.2
  366.4 5.4 copy.137
  371.8 5.4 copy.138
  377.1 8.4 constant_dynamic-update-slice_fusion.3
  386.8 9.4 fusion.76
  396.3 94.1 %reduce-scatter.10.cloned.1.call-done = f32[128,1024]{1,0:T(8,128)} async-done(((f32[2048,1024]{1,0:T(8,128)}), f32[128,1024]{1,0:T(8,128)}) %reduce-scatter.10.cloned.1.call-update) | async-done | bytes 524304 | tf_op jit(solution)/shard_map/reduce_scatter | solution.py:191
  490.4 1.2 copy.118
  491.9 3.9 fusion.78
  495.8 1.5 convolution_add_fusion.1
  497.3 101.4 %reduce-scatter.12.cloned.1.call-done = f32[128,1024]{1,0:T(8,128)} async-done(((f32[2048,1024]{1,0:T(8,128)}), f32[128,1024]{1,0:T(8,128)}) %reduce-scatter.12.cloned.1.call-update) | async-done | bytes 524304 | tf_op jit(solution)/shard_map/reduce_scatter | solution.py:194
  598.7 4.9 convolution_add_fusion
  603.7 4.5 fusion.55
  609.5 4.6 fusion.66
  614.1 4.7 fusion.64
  619.8 4.6 fusion.58
  625.4 14.5 fusion.79
  640.0 14.4 fusion.80
  655.7 13.2 fusion.81
  670.9 1.6 fusion.53
  672.5 62.3 %all-reduce.2 = (f32[2048]{0:T(1024)S(1)}, f32[2048]{0:T(1024)S(1)}) all-reduce(f32[2048]{0:T(1024)S(1)} %get-tuple-element.440, f32[2048]{0:T(1024)S(1)} %copy-done.30), channel_id=11, replica_groups=mesh['seq'=16,'head'=2] {'seq'}, use_global_device_ids=true, to_apply=%region_22.23.clone | all-reduce | flops 4096 | bytes 32768
  736.0 2.2 add_convert_fusion
  738.2 2.4 fusion.52
  740.5 36.3 %reduce-scatter.20.cloned.1.call-done = f32[1024,128]{1,0:T(8,128)} async-done(((f32[1024,2048]{1,0:T(8,128)}), f32[1024,128]{1,0:T(8,128)}) %reduce-scatter.20.cloned.1.call-update) | async-done | bytes 524304 | tf_op jit(solution)/shard_map/reduce_scatter | solution.py:232
  776.9 109.6 %reduce-scatter.14.cloned.1.call-done = f32[128,1024]{1,0:T(8,128)} async-done(((f32[2048,1024]{1,0:T(8,128)}), f32[128,1024]{1,0:T(8,128)}) %reduce-scatter.14.cloned.1.call-update) | async-done | bytes 524304 | tf_op jit(solution)/shard_map/reduce_scatter | solution.py:229
  886.5 109.5 %reduce-scatter.16.cloned.1.call-done = f32[128,1024]{1,0:T(8,128)} async-done(((f32[2048,1024]{1,0:T(8,128)}), f32[128,1024]{1,0:T(8,128)}) %reduce-scatter.16.cloned.1.call-update) | async-done | bytes 524304 | tf_op jit(solution)/shard_map/reduce_scatter | solution.py:230
  996.0 109.6 %reduce-scatter.18.cloned.1.call-done = f32[128,1024]{1,0:T(8,128)} async-done(((f32[2048,1024]{1,0:T(8,128)}), f32[128,1024]{1,0:T(8,128)}) %reduce-scatter.18.cloned.1.call-update) | async-done | bytes 524304 | tf_op jit(solution)/shard_map/reduce_scatter | solution.py:231
  1105.7 337.8 %reduce-scatter.22.cloned.1.call-done = f32[128,4096]{1,0:T(8,128)} async-done(((f32[2048,4096]{1,0:T(8,128)}), f32[128,4096]{1,0:T(8,128)}) %reduce-scatter.22.cloned.1.call-update) | async-done | bytes 2097168 | tf_op jit(solution)/shard_map/reduce_scatter | solution.py:233
  1443.5 337.1 %reduce-scatter.24.cloned.1.call-done = f32[128,4096]{1,0:T(8,128)} async-done(((f32[2048,4096]{1,0:T(8,128)}), f32[128,4096]{1,0:T(8,128)}) %reduce-scatter.24.cloned.1.call-update) | async-done | bytes 2097168 | tf_op jit(solution)/shard_map/reduce_scatter | solution.py:234
  1780.6 337.1 %reduce-scatter.26.cloned.1.call-done = f32[4096,128]{1,0:T(8,128)} async-done(((f32[4096,2048]{1,0:T(8,128)}), f32[4096,128]{1,0:T(8,128)}) %reduce-scatter.26.cloned.1.call-update) | async-done | bytes 2097168 | tf_op jit(solution)/shard_map/reduce_scatter | solution.py:235
  (147 shorter events, 24.0 us)
Async XLA Ops:
  7.2 5.7 copy-start.2
  7.2 5.7 copy-start.22
  7.2 65.5 %all-gather.5.cloned.1.call-start = ((), (), s32[]{:S(2)}) async-start(), calls=%async_computation.10 | async-start | bytes 4456448 | tf_op jit(solution)/shard_map/all_gather | solution.py:122
  8.5 8.1 copy-start.28
  8.6 4.3 copy-start.10
  15.8 4.8 copy-start.24
  16.6 107.6 %all-gather.3.cloned.1.call-start = ((), (), s32[]{:S(2)}) async-start(), calls=%async_computation.9 | async-start | bytes 4456448 | tf_op jit(solution)/shard_map/all_gather | solution.py:123
  20.4 163.5 %all-reduce.8.cloned.1.call-start = ((), (), s32[]{:S(2)}) async-start(), calls=%async_computation.11 | async-start | bytes 2097152 | tf_op jit(solution)/shard_map/psum | solution.py:133
  141.2 4.4 copy-start.17
  141.2 44.2 %copy-start.27 = (f32[2048]{0:T(1024)S(1)}, f32[2048]{0:T(1024)}, u32[]{:S(2)}) copy-start(f32[2048]{0:T(1024)} %param.26) | copy-start | bytes 24580
  145.2 150.4 %all-reduce.10.cloned.1.call-start = ((), (), s32[]{:S(2)}) async-start(), calls=%async_computation.12 | async-start | bytes 2097152 | tf_op jit(solution)/shard_map/psum | solution.py:153
  185.4 112.6 %copy-start.5 = (f32[128,2048]{1,0:T(8,128)}, f32[128,2048]{1,0:T(8,128)S(1)}, u32[]{:S(2)}) copy-start(f32[128,2048]{1,0:T(8,128)S(1)} %get-tuple-element.489) | copy-start | bytes 3145732
  185.6 9.8 copy-start.7
  195.4 9.5 copy-start.19
  219.3 23.5 %copy-start.16 = (bf16[128,4096]{1,0:T(8,128)(2,1)}, bf16[128,4096]{1,0:T(8,128)(2,1)S(1)}, u32[]{:S(2)}) copy-start(bf16[128,4096]{1,0:T(8,128)(2,1)S(1)} %get-tuple-element.492) | copy-start | bytes 3145732
  255.4 235.0 %reduce-scatter.10.cloned.1.call-start = ((), (), s32[]{:S(2)}) async-start(), calls=%async_computation.13 | async-start | bytes 8912896 | tf_op jit(solution)/shard_map/reduce_scatter | solution.py:191
  295.6 4.8 copy-start.9
  299.5 1.0 copy-start.12
  305.8 3.4 copy-start.4
  309.2 2.0 copy-start
  311.2 2.8 copy-start.1
  347.5 3.4 copy-start.4
  350.9 2.0 copy-start
  352.9 2.8 copy-start.1
  385.6 213.2 %reduce-scatter.12.cloned.1.call-start = ((), (), s32[]{:S(2)}) async-start(), calls=%async_computation.14 | async-start | bytes 8912896 | tf_op jit(solution)/shard_map/reduce_scatter | solution.py:194
  385.6 1.2 copy-start.14
  386.1 284.7 %all-reduce.12.cloned.1.call-start = ((), (), s32[]{:S(2)}) async-start(), calls=%async_computation.22 | async-start | bytes 4194304 | tf_op jit(solution)/shard_map/psum | solution.py:141
  386.8 104.9 %copy-start.25 = (f32[128,64]{0,1:T(8,128)S(1)}, f32[128,64]{0,1:T(8,128)}, u32[]{:S(2)}) copy-start(f32[128,64]{0,1:T(8,128)} %get-tuple-element.507) | copy-start | bytes 98308
  386.8 104.9 %copy-start.26 = (f32[128,64]{0,1:T(8,128)S(1)}, f32[128,64]{0,1:T(8,128)}, u32[]{:S(2)}) copy-start(f32[128,64]{0,1:T(8,128)} %get-tuple-element.509) | copy-start | bytes 98308
  491.7 4.1 copy-start.11
  497.3 106.4 %copy-start.13 = (f32[128,2048]{1,0:T(8,128)S(1)}, f32[128,2048]{1,0:T(8,128)}, u32[]{:S(2)}) copy-start(f32[128,2048]{1,0:T(8,128)} %copy-done.12) | copy-start | bytes 3145732
  497.3 106.4 %copy-start.18 = (bf16[128,8,128]{0,2,1:T(8,128)(2,1)S(1)}, bf16[128,8,128]{0,2,1:T(8,128)(2,1)}, u32[]{:S(2)}) copy-start(bf16[128,8,128]{0,2,1:T(8,128)(2,1)} %copy-done.17) | copy-start | bytes 786436
  603.6 173.2 %reduce-scatter.20.cloned.1.call-start = ((), (), s32[]{:S(2)}) async-start(), calls=%async_computation.18 | async-start | bytes 8912896 | tf_op jit(solution)/shard_map/reduce_scatter | solution.py:232
  608.3 1.2 copy-start.3
  608.3 1.2 copy-start.23
  608.3 1.2 copy-start.29
  608.3 278.2 %reduce-scatter.14.cloned.1.call-start = ((), (), s32[]{:S(2)}) async-start(), calls=%async_computation.15 | async-start | bytes 8912896 | tf_op jit(solution)/shard_map/reduce_scatter | solution.py:229
  614.1 382.0 %reduce-scatter.16.cloned.1.call-start = ((), (), s32[]{:S(2)}) async-start(), calls=%async_computation.16 | async-start | bytes 8912896 | tf_op jit(solution)/shard_map/reduce_scatter | solution.py:230
  618.8 1.0 copy-start.21
  618.8 486.9 %reduce-scatter.18.cloned.1.call-start = ((), (), s32[]{:S(2)}) async-start(), calls=%async_computation.17 | async-start | bytes 8912896 | tf_op jit(solution)/shard_map/reduce_scatter | solution.py:231
  624.4 1.0 copy-start.8
  624.4 819.1 %reduce-scatter.22.cloned.1.call-start = ((), (), s32[]{:S(2)}) async-start(), calls=%async_computation.19 | async-start | bytes 35651584 | tf_op jit(solution)/shard_map/reduce_scatter | solution.py:233
  639.9 1140.7 %reduce-scatter.24.cloned.1.call-start = ((), (), s32[]{:S(2)}) async-start(), calls=%async_computation.20 | async-start | bytes 35651584 | tf_op jit(solution)/shard_map/reduce_scatter | solution.py:234
  654.4 1.2 copy-start.15
  654.4 1.4 copy-start.20
  654.4 1463.3 %reduce-scatter.26.cloned.1.call-start = ((), (), s32[]{:S(2)}) async-start(), calls=%async_computation.21 | async-start | bytes 35651584 | tf_op jit(solution)/shard_map/reduce_scatter | solution.py:235
  668.9 0.7 copy-start.31
  668.9 3.5 copy-start.30
  668.9 67.0 %copy-start.6 = (f32[128,2048]{1,0:T(8,128)S(1)}, f32[128,2048]{1,0:T(8,128)}, u32[]{:S(2)}) copy-start(f32[128,2048]{1,0:T(8,128)} %copy-done.5) | copy-start | bytes 3145732
Sparse Core Ops, SparseCore 0:
  16.7 55.9 all-gather.4
  75.4 48.7 all-gather.2
  145.4 38.5 all-reduce.7
  255.5 40.0 all-reduce.9
  385.7 104.7 reduce-scatter.9
  494.3 104.3 reduce-scatter.11
  603.8 62.8 all-reduce.11
  671.8 104.9 reduce-scatter.19
  782.1 104.4 reduce-scatter.13
  891.6 104.4 reduce-scatter.15
  1001.2 104.4 reduce-scatter.17
  1110.9 332.4 reduce-scatter.21
  1448.9 331.6 reduce-scatter.23
  1785.9 331.7 reduce-scatter.25
where the time goes:
time: 2130 us; the launch traced here: 2120 us
  waiting for transfers between devices  1750 us (82%)
  matrix products  199 us (9%)
  local copies, waits for them, and re-layouts  70.3 us (3%)
  blocking collectives  62.3 us (3%)
    reduce_scatter x1, waiting for transfers between devices, local(): lax.psum_scatter(gate_term, 'seq', scatter_dimension=0, tiled=True)  338 us
    reduce_scatter x1, waiting for transfers between devices, local(): lax.psum_scatter(upward_term, 'seq', scatter_dimension=0, tiled=True)  337 us
    reduce_scatter x1, waiting for transfers between devices, local(): lax.psum_scatter(down_term, 'seq', scatter_dimension=1, tiled=True)  337 us
    reduce_scatter x1, waiting for transfers between devices, local(): lax.psum_scatter(value_term, 'seq', scatter_dimension=0, tiled=True)  110 us
    reduce_scatter x1, waiting for transfers between devices, local(): lax.psum_scatter(query_term, 'seq', scatter_dimension=0, tiled=True)  110 us
    reduce_scatter x1, waiting for transfers between devices, local(): lax.psum_scatter(key_term, 'seq', scatter_dimension=0, tiled=True)  109 us
    reduce_scatter x1, waiting for transfers between devices, local(): lax.psum_scatter(value_parts.reshape(total_rows, local_width), 'seq', sca...  101 us
    reduce_scatter x1, waiting for transfers between devices, local(): lax.psum_scatter(key_parts.reshape(total_rows, local_width), 'seq', scatt...  94.1 us
  transfers between devices with their start and end apart: 14, of which 13 were waited for; matrix products, arithmetic and copies ran while one was open for 4% of the time, Pallas kernels for 0%

commit v1 on v0

v1 whole, which is shorter than its diff:
```python
import math

import jax
import jax.numpy as jnp
from jax import lax
from jax.sharding import PartitionSpec as P

HD = 128
BIAS_LEN = 4096
BF16 = jnp.bfloat16
F32 = jnp.float32


def frequencies(head_dim):
    half_dim = head_dim // 2
    return jnp.exp(-jnp.arange(half_dim).astype(F32) * (2.0 / head_dim) * math.log(10000.0))


def turned(values, angles):
    half_dim = values.shape[-1] // 2
    cosine = jnp.cos(angles)[:, None, :]
    sine = jnp.sin(angles)[:, None, :]
    former = values[..., :half_dim]
    latter = values[..., half_dim:]
    return jnp.concatenate(
        [former * cosine - latter * sine, former * sine + latter * cosine], axis=-1
    )


def normalized(values, gain):
    inverse = lax.rsqrt(jnp.mean(values * values, axis=-1, keepdims=True) + 1e-05)
    return values * inverse * gain, inverse


def norm_back(values, inverse, gain, upstream):
    scaled = values * inverse
    weighted = upstream * gain
    return inverse * (weighted - scaled * jnp.mean(weighted * scaled, axis=-1, keepdims=True))


def dot(one, two):
    return jnp.dot(one, two, preferred_element_type=F32)


def dot_rows(one, two):
    return lax.dot_general(one, two, (((0,), (0,)), ((), ())), preferred_element_type=F32)


def dot_back(one, two):
    return lax.dot_general(one, two, (((1,), (1,)), ((), ())), preferred_element_type=F32)


def local(
    activations,
    doc_ids,
    w_query,
    w_key,
    w_value,
    w_out,
    w_gate,
    w_up,
    w_down,
    gain_attn,
    gain_mlp,
    cotangent,
):
    rows, width = activations.shape
    devices = lax.axis_size("seq")
    total = rows * devices
    features = width // devices
    local_width = w_query.shape[1]
    heads = local_width // HD
    share = devices // (2 * heads)
    me = lax.axis_index("seq")
    core = me % 2
    residue = (me // 2) % share
    head = me // (2 * share)
    hidden = w_gate.shape[1] // 2

    def place(a, r, c):
        return (a * share + r) * 2 + c

    def split(s):
        return s // (2 * share), (s // 2) % share, s % 2

    def permuted(x, target):
        return lax.ppermute(x, "seq", [(s, target(*split(s))) for s in range(devices)])

    def core_swap(x):
        return permuted(x, lambda a, r, c: place(a, r, 1 - c))

    def pair_swap(x):
        return permuted(x, lambda a, r, c: place(a ^ 1, r, c))

    def ring_step(x):
        return permuted(x, lambda a, r, c: place((a + 2) % heads, r, c))

    def head_swap(x):
        return lax.ppermute(x, "head", [(0, 1), (1, 0)])

    head_groups = [
        [place(a, r, c) for a in range(heads)] for r in range(share) for c in range(2)
    ]
    share_groups = [
        [place(a, r, c) for r in range(share)] for a in range(heads) for c in range(2)
    ]

    def exchange(x):
        return lax.all_to_all(x, "seq", 0, 0, tiled=True, axis_index_groups=head_groups)

    def share_sum(x, dim):
        if share == 1:
            return x
        return lax.psum_scatter(
            x, "seq", scatter_dimension=dim, tiled=True, axis_index_groups=share_groups
        )

    def in_core_order(mine, other, axis):
        stacked = jnp.stack([mine, other], axis)
        return jnp.where(core == 0, stacked, jnp.flip(stacked, axis))

    def my_part(x, index, axis):
        return lax.dynamic_index_in_dim(x, index, axis, keepdims=False)

    my_places = me * rows + jnp.arange(rows, dtype=jnp.int32)
    angles = my_places.astype(F32)[:, None] * frequencies(HD)[None, :]
    block_starts = place(jnp.arange(heads, dtype=jnp.int32), residue, core) * rows
    query_places = (block_starts[:, None] + jnp.arange(rows, dtype=jnp.int32)[None, :]).reshape(-1)
    query_angles = query_places.astype(F32)[:, None] * frequencies(HD)[None, :]
    query_docs = doc_ids.reshape(heads, share, 2, rows)[:, residue, core].reshape(-1)
    allowed = (query_docs[:, None] == doc_ids[None, :]) & (
        jnp.arange(total, dtype=jnp.int32)[None, :] <= query_places[:, None]
    )
    scale = HD ** (-0.5)

    inputs = activations.astype(F32)
    normed, inverse_attn = normalized(inputs, gain_attn)
    normed_low = normed.astype(BF16)
    query = turned(dot(normed_low, w_query).reshape(rows, heads, HD), angles).astype(BF16)
    key = turned(dot(normed_low, w_key).reshape(rows, heads, HD), angles).astype(BF16)
    value = dot(normed_low, w_value).astype(BF16).reshape(rows, heads, HD)
    sent = jnp.concatenate([query, key, value], -1).transpose(1, 0, 2)
    received = exchange(sent)
    head_query = received[:, :, :HD].reshape(heads * rows, HD)
    own_kv = received[:, :, HD:]

    def all_keys(own):
        if share > 1:
            own = lax.all_gather(own, "seq", axis=1, axis_index_groups=share_groups)
        else:
            own = own[:, None]
        return in_core_order(own, core_swap(own), 2).reshape(total, 2 * HD)

    head_kv = all_keys(own_kv)
    head_key, head_value = head_kv[:, :HD], head_kv[:, HD:]
    weights = jnp.where(
        allowed, jax.nn.sigmoid(dot_back(head_query, head_key) * scale - math.log(BIAS_LEN)), 0.0
    )
    head_mixed = dot(weights.astype(BF16), head_value).astype(BF16)
    attended = exchange(head_mixed.reshape(heads, rows, HD)).transpose(1, 0, 2).reshape(rows, -1)

    def gathered(x):
        blocks = [x]
        for _ in range(heads // 2 - 1):
            blocks.append(ring_step(blocks[-1]))
        return blocks

    branch = dot(attended, w_out).astype(BF16)
    branch = branch.astype(F32) + head_swap(branch).astype(F32)
    middle = inputs + branch
    second, inverse_mlp = normalized(middle, gain_mlp)
    second_low = second.astype(BF16)

    gate_w = lax.dynamic_slice_in_dim(w_gate, core * hidden, hidden, 1)
    up_w = lax.dynamic_slice_in_dim(w_up, core * hidden, hidden, 1)
    down_w = lax.dynamic_slice_in_dim(w_down, core * hidden, hidden, 0)

    def feed_forward(normed_rows, grad_rows):
        gate = dot(normed_rows, gate_w)
        upward = dot(normed_rows, up_w)
        gate_sig = jax.nn.sigmoid(gate)
        hidden_low = (gate * gate_sig * upward).astype(BF16)
        hidden_grad = dot_back(grad_rows, down_w)
        gate_low = (hidden_grad * upward * gate_sig * (1.0 + gate * (1.0 - gate_sig))).astype(BF16)
        upward_low = (hidden_grad * gate * gate_sig).astype(BF16)
        return hidden_low, gate_low, upward_low

    chip_second = jnp.concatenate([second_low, core_swap(second_low)], 0)
    chip_cotangent = jnp.concatenate([cotangent, core_swap(cotangent)], 0)
    hidden_low, gate_low, upward_low = feed_forward(chip_second, chip_cotangent)
    second_part = dot_back(gate_low, gate_w) + dot_back(upward_low, up_w)

    def chip_sum(part):
        part = part[:rows] + core_swap(part[rows:].astype(BF16)).astype(F32)
        part = part.astype(BF16)
        return part.astype(F32) + head_swap(part).astype(F32)

    second_grad = chip_sum(second_part)
    output = (middle + chip_sum(dot(hidden_low, down_w))).astype(BF16)
    grad_out = cotangent.astype(F32)
    middle_grad = grad_out + norm_back(middle, inverse_mlp, gain_mlp, second_grad)
    branch_low = middle_grad.astype(BF16)

    mixed_grad = dot_back(branch_low, w_out).astype(BF16)
    head_mixed_grad = exchange(mixed_grad.reshape(rows, heads, HD).transpose(1, 0, 2)).reshape(
        heads * rows, HD
    )
    weights = jnp.where(
        allowed, jax.nn.sigmoid(dot_back(head_query, head_key) * scale - math.log(BIAS_LEN)), 0.0
    )
    value_part = dot_rows(weights.astype(BF16), head_mixed_grad)
    score_grad = (dot_back(head_mixed_grad, head_value) * weights * (1.0 - weights)).astype(BF16)
    query_grad = dot(score_grad, head_key) * scale
    key_part = dot_rows(score_grad, head_query) * scale
    parts = jnp.concatenate([key_part, value_part], 1).reshape(heads, share, 2, rows, 2 * HD)
    own_part = my_part(parts, core, 2) + core_swap(my_part(parts, 1 - core, 2).astype(BF16)).astype(
        F32
    )
    own_part = share_sum(own_part, 1).reshape(heads * rows, 1, 2 * HD)
    turned_back = turned(
        jnp.concatenate([query_grad[:, None], own_part[..., :HD]], 1), -query_angles
    )
    head_grads = jnp.concatenate(
        [turned_back.reshape(heads * rows, 2 * HD), own_part[:, 0, HD:]], 1
    ).astype(BF16)
    row_grads = exchange(head_grads.reshape(heads, rows, 3 * HD))
    row_grads = row_grads.reshape(heads, rows, 3, HD).transpose(2, 1, 0, 3).reshape(3, rows, -1)
    normed_part = (
        dot_back(row_grads[0], w_query)
        + dot_back(row_grads[1], w_key)
        + dot_back(row_grads[2], w_value)
    ).astype(BF16)
    normed_grad = normed_part.astype(F32) + head_swap(normed_part).astype(F32)
    input_grad = (middle_grad + norm_back(inputs, inverse_attn, gain_attn, normed_grad)).astype(BF16)

    def plane_tokens(x):
        blocks = gathered(x)
        return jnp.concatenate(blocks + [core_swap(block) for block in blocks], 0)

    plane_second = plane_tokens(second_low)
    plane_cotangent = plane_tokens(cotangent)
    plane_rows = 4 * share * features
    plane_start = (head // 2) * plane_rows
    hidden_low, gate_low, upward_low = feed_forward(plane_second, plane_cotangent)
    second_rows = lax.dynamic_slice_in_dim(plane_second, plane_start, plane_rows, 1)
    cotangent_rows = lax.dynamic_slice_in_dim(plane_cotangent, plane_start, plane_rows, 1)

    def weight_sum(partial, axis):
        shape = partial.shape
        partial = partial.reshape(shape[:axis] + (2, share * 2 * features) + shape[axis + 1 :])
        mine, other = my_part(partial, head % 2, axis), my_part(partial, 1 - head % 2, axis)
        mine = share_sum(mine + pair_swap(other.astype(BF16)).astype(F32), axis)
        mine = mine.reshape(shape[:axis] + (2, features) + shape[axis + 1 :])
        kept, given = my_part(mine, core, axis), my_part(mine, 1 - core, axis)
        both = in_core_order(kept, core_swap(given.astype(BF16)).astype(F32), 1 - axis)
        return both.reshape((features, -1) if axis == 0 else (-1, features))

    gate_sum = weight_sum(dot_rows(second_rows, gate_low), 0)
    up_sum = weight_sum(dot_rows(second_rows, upward_low), 0)
    down_sum = weight_sum(dot_rows(hidden_low, cotangent_rows), 1)

    def head_tokens(x):
        blocks = gathered(x)
        blocks = blocks + [pair_swap(block) for block in blocks]
        return blocks

    def source(index):
        ring = heads // 2
        step, paired = index % ring, index // ring
        return (head - 2 * step) % heads ^ paired

    order = jnp.stack([source(index) for index in range(heads)])

    def in_token_order(x):
        return jnp.take(x.reshape((heads, rows) + x.shape[1:]), order, axis=0).reshape(x.shape)

    def shared_sum(partial, axis):
        shape = partial.shape
        parts = partial.reshape(shape[:axis] + (heads, share, 2, features) + shape[axis + 1 :])
        mine = my_part(parts, core, axis + 2) + core_swap(
            my_part(parts, 1 - core, axis + 2).astype(BF16)
        ).astype(F32)
        return share_sum(mine, axis + 1).reshape(
            shape[:axis] + (heads, features) + shape[axis + 1 :]
        )

    all_normed = jnp.concatenate(head_tokens(normed_low), 0)
    head_sum = shared_sum(dot_rows(all_normed, in_token_order(head_grads)), 0)
    row_sum = exchange(head_sum.astype(BF16)).astype(F32)
    row_sum = row_sum.reshape(heads, features, 3, HD).transpose(2, 1, 0, 3).reshape(3, features, -1)

    all_attended = jnp.concatenate(head_tokens(attended), 0)
    chip_columns = width // heads
    sent_branch = exchange(branch_low.reshape(rows, heads, chip_columns).transpose(1, 0, 2))
    out_part = dot_rows(all_attended, in_token_order(sent_branch.reshape(heads * rows, -1)))
    out_part = out_part.reshape(local_width, share, 2, features)
    out_sum = my_part(out_part, core, 2) + core_swap(
        my_part(out_part, 1 - core, 2).astype(BF16)
    ).astype(F32)
    out_sum = share_sum(out_sum, 1).reshape(local_width, features)

    my_start = me * features

    def gain_sum(pairs, gain):
        term = 0.0
        for weight, grad in pairs:
            own = lax.dynamic_slice_in_dim(weight, my_start, features, 0).astype(F32)
            term = term + jnp.sum(own * grad, axis=1)
        return term / lax.dynamic_slice_in_dim(gain, my_start, features, 0)

    gains = jnp.stack(
        [
            gain_sum(((w_query, row_sum[0]), (w_key, row_sum[1]), (w_value, row_sum[2])), gain_attn),
            gain_sum(((w_gate, gate_sum), (w_up, up_sum)), gain_mlp),
        ]
    )
    gains = gains + head_swap(gains)
    return (
        output,
        input_grad,
        row_sum[0],
        row_sum[1],
        row_sum[2],
        out_sum,
        gate_sum,
        up_sum,
        down_sum,
        gains[0],
        gains[1],
    )


def solution(mesh):
    placed = (
        P("seq", None),
        P(),
        P(None, "head"),
        P(None, "head"),
        P(None, "head"),
        P("head", None),
        P(None, "head"),
        P(None, "head"),
        P("head", None),
        P(),
        P(),
        P("seq", None),
    )
    return jax.shard_map(
        local,
        mesh=mesh,
        in_specs=placed,
        out_specs=(
            P("seq", None),
            P("seq", None),
            P("seq", "head"),
            P("seq", "head"),
            P("seq", "head"),
            P("head", "seq"),
            P("seq", "head"),
            P("seq", "head"),
            P("head", "seq"),
            P("seq"),
            P("seq"),
        ),
        check_vma=False,
    )
```

time: 2130 us -> 526 us (0.25)
  waiting for transfers between devices: 1750 us -> 137 us
  starting transfers between devices: 1.3 us -> 65.9 us
  blocking collectives: 62.3 us -> 0 us
  matrix products: 199 us -> 145 us
  local copies, waits for them, and re-layouts: 70.3 us -> 115 us
  other arithmetic: 18.9 us -> 51.8 us
    reduce_scatter x9 -> x0, waiting for transfers between devices: 1570 us -> none  [the longest x1 338 us: local(): lax.psum_scatter(gate_term, 'seq', scatter_dimension=0, tiled=True)]
    ppermute x0 -> x45, waiting for transfers between devices: none -> 116 us  [the longest x40 93.3 us: permuted(): lax.ppermute(x, 'seq', [(s, target(*split(s))) for s in range(devices)])]
    all_gather x2 -> x0, waiting for transfers between devices: 97 us -> none  [the longest x1 51.9 us: local(): lax.all_gather(key_rot, 'seq', axis=0, tiled=True)]
    psum x3 -> x0, waiting for transfers between devices: 78.5 us -> none  [the longest x1 40.1 us: local(): second_grad = lax.psum(second_part, 'head')]
    unnamed x1 -> x0, blocking collectives: 62.3 us -> none
    dot_general x31 -> x28, matrix products: 193 us -> 145 us  [the longest x11 53.9 us: dot(): return jnp.dot(one, two, preferred_element_type=F32)]
    ppermute x0 -> x45, starting transfers between devices: none -> 38.9 us  [the longest x40 34 us: permuted(): lax.ppermute(x, 'seq', [(s, target(*split(s))) for s in range(devices)])]
    dynamic_update_slice x6 -> x0, local copies, waits for them, and re-layouts: 38.3 us -> none  [local(): lax.scan(back_block, empty_out, key_starts)]
  transfers between devices with their start and end apart: 14 -> 51, of which waited for: 13 -> 15; matrix products, arithmetic and copies ran while one was open for 4% -> 57% of each run, Pallas kernels for 0% -> 0%
where the time goes in v1:
time: 526 us; the launch traced here: 517 us
  matrix products  145 us (28%)
  waiting for transfers between devices  137 us (26%)
  local copies, waits for them, and re-layouts  115 us (22%)
  starting transfers between devices  65.9 us (13%)
  other arithmetic  51.8 us (10%)
    ppermute x40, waiting for transfers between devices, permuted(): lax.ppermute(x, 'seq', [(s, target(*split(s))) for s in range(devices)])  93.3 us
    dot_general x11, matrix products, dot(): return jnp.dot(one, two, preferred_element_type=F32)  53.9 us
    dot_general x10, matrix products, dot_back(): lax.dot_general(one, two, (((1,), (1,)), ((), ())), preferred_element_typ...  50.6 us
    unnamed x149, local copies, waits for them, and re-layouts  47.8 us
    dot_general x7, matrix products, dot_rows(): lax.dot_general(one, two, (((0,), (0,)), ((), ())), preferred_element_typ...  40.4 us
    ppermute x40, starting transfers between devices, permuted(): lax.ppermute(x, 'seq', [(s, target(*split(s))) for s in range(devices)])  34 us
    all_to_all x6, starting transfers between devices, exchange(): lax.all_to_all(x, 'seq', 0, 0, tiled=True, axis_index_groups=head_groups)  27 us
    ppermute x5, waiting for transfers between devices, head_swap(): return lax.ppermute(x, 'head', [(0, 1), (1, 0)])  22.4 us
  transfers between devices with their start and end apart: 51, of which 15 were waited for; matrix products, arithmetic and copies ran while one was open for 57% of the time, Pallas kernels for 0%

profile of v1, /device:TPU:0, one launch (start us, length us, event | category | flops | bytes accessed | tf_op | source)
XLA Modules:
  0.0 516.9 jit_solution(5272332991171970025)
XLA Ops:
  1.2 2.6 collective-permute-start.32
  5.0 2.0 constant_dynamic-update-slice_fusion.7
  10.2 3.1 fusion.39
  18.7 3.5 all-to-all-start
  26.7 2.0 collective-permute-start.33
  31.9 2.5 collective-permute-start.11
  34.4 7.1 %fusion.3 = f32[256,2048]{1,0:T(8,128)} fusion(bf16[4096,2048]{1,0:T(8,128)(2,1)} %param.20, s32[]{:T(128)S(6)} %select_n.183, bf16[128,2048]{1,0:T(8,128)(2,1)S(1)} %collective-permute-done.5, bf16[128,2048]{1,0:T(8,128)(2,1)S(1)} %copy-done.28), kind=kOutput, calls=%fused_computation.12 | convolution fusion | flops 2149580800 | bytes 11534340 | tf_op jit(solution)/shard_map/dot_general | solution.py:50
  45.3 9.0 %collective-permute-done.33 = bf16[128,2048]{1,0:T(8,128)(2,1)} collective-permute-done((bf16[128,2048]{1,0:T(8,128)(2,1)}, bf16[128,2048]{1,0:T(8,128)(2,1)}, u32[]{:S(2)}, u32[]{:S(2)}) %collective-permute-start.33) | collective-permute-done | bytes 524320 | tf_op jit(solution)/shard_map/ppermute | solution.py:87
  54.3 3.0 collective-permute-start.34
  59.2 6.2 %collective-permute-done.11 = bf16[128,2048]{1,0:T(8,128)(2,1)S(1)} collective-permute-done((bf16[128,2048]{1,0:T(8,128)(2,1)}, bf16[128,2048]{1,0:T(8,128)(2,1)S(1)}, u32[]{:S(2)}, u32[]{:S(2)}) %collective-permute-start.11) | collective-permute-done | bytes 524320 | tf_op jit(solution)/shard_map/ppermute | solution.py:87
  67.1 13.3 %all-to-all-done = bf16[8,128,384]{2,1,0:T(8,128)(2,1)S(1)} async-done(((bf16[8,128,384]{2,1,0:T(8,128)(2,1)}), bf16[8,128,384]{2,1,0:T(8,128)(2,1)S(1)}, u32[]{:S(2)}, u32[]{:S(2)}) %all-to-all-start) | async-done | bytes 786464 | tf_op jit(solution)/shard_map/all_to_all | solution.py:109
  89.0 7.8 %collective-permute-done.12 = bf16[128,2048]{1,0:T(8,128)(2,1)} collective-permute-done((bf16[128,2048]{1,0:T(8,128)(2,1)}, bf16[128,2048]{1,0:T(8,128)(2,1)}, u32[]{:S(2)}, u32[]{:S(2)}) %collective-permute-start.12) | collective-permute-done | bytes 524320 | tf_op jit(solution)/shard_map/ppermute | solution.py:87
  103.4 3.3 divide_select_fusion
  106.7 2.5 fusion.36
  110.0 3.4 all-to-all-start.1
  116.2 6.8 %all-to-all-done.1 = bf16[8,128,128]{2,1,0:T(8,128)(2,1)S(1)} async-done(((bf16[8,128,128]{2,1,0:T(8,128)(2,1)}), bf16[8,128,128]{2,1,0:T(8,128)(2,1)S(1)}, u32[]{:S(2)}, u32[]{:S(2)}) %all-to-all-start.1) | async-done | bytes 262176 | tf_op jit(solution)/shard_map/all_to_all | solution.py:109
  124.3 3.1 convolution_convert_fusion
  129.0 13.2 %fusion.1 = f32[1024,2048]{1,0:T(8,128)} fusion(bf16[1024,2048]{1,0:T(8,128)(2,1)S(1)} %copy-done.42, bf16[4096,2048]{1,0:T(8,128)(2,1)} %param.20, s32[]{:T(128)S(6)} %select_n.183), kind=kOutput, calls=%fused_computation.10 | convolution fusion | flops 8589934592 | bytes 20971524 | tf_op jit(solution)/shard_map/dot_general | solution.py:50
  143.3 6.5 %copy.82 = bf16[2048,1024]{1,0:T(8,128)(2,1)} copy(bf16[2048,1024]{0,1:T(8,128)(2,1)} %bitcast.24) | data formatting | bytes 8388608 | tf_op jit(solution)/shard_map/reshape.206
  152.4 2.2 collective-permute-start.20
  156.4 4.4 collective-permute-done.20
  164.7 5.5 %collective-permute-done.23 = bf16[128,1024]{0,1:T(8,128)(2,1)S(1)} collective-permute-done((bf16[128,1024]{0,1:T(8,128)(2,1)}, bf16[128,1024]{0,1:T(8,128)(2,1)S(1)}, u32[]{:S(2)}, u32[]{:S(2)}) %collective-permute-start.23) | collective-permute-done | bytes 262176 | tf_op jit(solution)/shard_map/ppermute | solution.py:87
  170.4 6.0 %fusion.17 = f32[256,2048]{1,0:T(8,128)S(1)} fusion(bf16[2048,4096]{1,0:T(8,128)(2,1)} %param.18, s32[]{:T(128)S(6)} %select_n.183, bf16[128,2048]{1,0:T(8,128)(2,1)S(1)} %collective-permute-done.2, bf16[128,2048]{1,0:T(8,128)(2,1)S(1)} %get-tuple-element.34), kind=kOutput, calls=%fused_computation.26 | convolution fusion | flops 2149580800 | bytes 11534340 | tf_op jit(solution)/shard_map/dot_general | solution.py:42
  176.4 7.2 %fusion.9 = f32[256,2048]{1,0:T(8,128)} fusion(bf16[2048,4096]{1,0:T(8,128)(2,1)} %param.19, s32[]{:T(128)S(6)} %select_n.183, f32[256,2048]{1,0:T(8,128)S(1)} %copy-done.52, f32[256,2048]{1,0:T(8,128)S(1)} %fusion.17), kind=kOutput, calls=%fused_computation.18 | convolution fusion | flops 2150629376 | bytes 14680068 | tf_op jit(solution)/shard_map/dot_general | solution.py:50
  183.6 5.7 %fusion.11 = f32[256,2048]{1,0:T(8,128)S(1)} fusion(bf16[2048,4096]{1,0:T(8,128)(2,1)} %param.19, s32[]{:T(128)S(6)} %select_n.183, bf16[128,2048]{1,0:T(8,128)(2,1)S(1)} %collective-permute-done.2, bf16[128,2048]{1,0:T(8,128)(2,1)S(1)} %get-tuple-element.34), kind=kOutput, calls=%fused_computation.20 | convolution fusion | flops 2149580800 | bytes 11534340 | tf_op jit(solution)/shard_map/dot_general | solution.py:42
  189.3 6.8 %fusion.22 = f32[256,2048]{1,0:T(8,128)S(1)} fusion(f32[256,2048]{1,0:T(8,128)} %fusion.9, bf16[2048,4096]{1,0:T(8,128)(2,1)} %param.18, s32[]{:T(128)S(6)} %select_n.183, f32[256,2048]{1,0:T(8,128)S(1)} %fusion.17, f32[256,2048]{1,0:T(8,128)S(1)} %copy-done.52, f32[256,2048]{1,0:T(8,128)S(1)} %fusion.11), kind=kOutput, calls=%fused_computation.32 | convolution fusion | flops 2153250816 | bytes 18874372 | tf_op jit(solution)/shard_map/dot_general | solution.py:50
  196.2 5.9 %fusion.5 = f32[256,2048]{1,0:T(8,128)S(1)} fusion(bf16[4096,2048]{1,0:T(8,128)(2,1)} %param.20, s32[]{:T(128)S(6)} %select_n.183, f32[256,2048]{1,0:T(8,128)S(1)} %fusion.11, f32[256,2048]{1,0:T(8,128)S(1)} %fusion.17), kind=kOutput, calls=%fused_computation.14 | convolution fusion | flops 2150629376 | bytes 14680068 | tf_op jit(solution)/shard_map/dot_general | solution.py:42
  207.6 11.7 %collective-permute-done.27 = bf16[128,2048]{1,0:T(8,128)(2,1)} collective-permute-done((bf16[128,2048]{1,0:T(8,128)(2,1)}, bf16[128,2048]{1,0:T(8,128)(2,1)}, u32[]{:S(2)}, u32[]{:S(2)}) %collective-permute-start.27) | collective-permute-done | bytes 524320 | tf_op jit(solution)/shard_map/ppermute | solution.py:87
  221.1 9.5 %collective-permute-done.4 = bf16[128,2048]{1,0:T(8,128)(2,1)S(1)} collective-permute-done((bf16[128,2048]{1,0:T(8,128)(2,1)S(1)}, bf16[128,2048]{1,0:T(8,128)(2,1)S(1)}, u32[]{:S(2)}, u32[]{:S(2)}) %collective-permute-start.4) | collective-permute-done | bytes 524320 | tf_op jit(solution)/shard_map/ppermute | solution.py:99
  230.6 2.0 fusion.99
  234.9 4.3 all-to-all-start.2
  247.7 4.8 all-to-all-start.5
  252.5 4.1 fusion.28
  256.7 4.6 multiply_convert_fusion.3
  261.3 2.0 copy-done.1
  265.6 3.0 reshape.733
  268.6 2.8 constant_dynamic-slice_fusion.4
  275.2 13.3 %fusion.13 = f32[1024,2048]{1,0:T(8,128)} fusion(bf16[1024,2048]{1,0:T(8,128)(2,1)S(1)} %constant_dynamic-update-slice_fusion.16, bf16[2048,4096]{1,0:T(8,128)(2,1)} %param.18, s32[]{:T(128)S(6)} %select_n.183), kind=kOutput, calls=%fused_computation.22 | convolution fusion | flops 8589934592 | bytes 20971524 | tf_op jit(solution)/shard_map/dot_general | solution.py:42
  288.5 11.3 %fusion.7 = f32[1024,2048]{1,0:T(8,128)} fusion(bf16[1024,2048]{1,0:T(8,128)(2,1)S(1)} %constant_dynamic-update-slice_fusion.16, bf16[2048,4096]{1,0:T(8,128)(2,1)S(1)} %bitcast.238, s32[]{:T(128)S(6)} %select_n.183), kind=kOutput, calls=%fused_computation.16 | convolution fusion | flops 8589934592 | bytes 20971524 | tf_op jit(solution)/shard_map/dot_general | solution.py:42
  299.8 7.7 %fusion.20 = f32[2048,512]{0,1:T(8,128)S(1)} fusion(f32[1024,2048]{1,0:T(8,128)} %fusion.7, f32[1024,2048]{1,0:T(8,128)} %fusion.13, bf16[1024,2048]{1,0:T(8,128)(2,1)} %constant_dynamic-update-slice_fusion.24, s32[]{:T(128)S(6)} %select_n.197), kind=kOutput, calls=%fused_computation.29 | convolution fusion | flops 2160066560 | bytes 22020100 | tf_op jit(solution)/shard_map/dot_general | solution.py:46
  307.5 11.9 %fusion.21 = f32[512,2048]{1,0:T(8,128)S(1)} fusion(f32[1024,2048]{1,0:T(8,128)} %fusion.13, f32[1024,2048]{1,0:T(8,128)} %fusion.1, f32[1024,2048]{1,0:T(8,128)} %fusion.7, bf16[1024,2048]{1,0:T(8,128)(2,1)S(1)} %constant_dynamic-update-slice_fusion.16, s32[]{:T(128)S(6)} %select_n.197), kind=kOutput, calls=%fused_computation.30 | convolution fusion | flops 2168455168 | bytes 30408708 | tf_op jit(solution)/shard_map/dot_general | solution.py:46
  319.4 8.8 %fusion.19 = f32[512,2048]{1,0:T(8,128)S(1)} fusion(f32[1024,2048]{1,0:T(8,128)} %fusion.1, f32[1024,2048]{1,0:T(8,128)} %fusion.13, bf16[1024,2048]{1,0:T(8,128)(2,1)S(1)} %constant_dynamic-update-slice_fusion.16, s32[]{:T(128)S(6)} %select_n.197), kind=kOutput, calls=%fused_computation.28 | convolution fusion | flops 2160066560 | bytes 22020100 | tf_op jit(solution)/shard_map/dot_general | solution.py:46
  329.7 2.0 collective-permute-start.42
  338.9 2.4 fusion.26
  346.6 4.8 all-to-all-start.3
  351.4 2.0 gather_fusion
  353.7 4.7 fusion.105
  359.5 2.1 add_bitcast_fusion
  361.6 45.6 %collective-permute-done.38 = bf16[256,2048]{1,0:T(8,128)(2,1)} collective-permute-done((bf16[256,2048]{1,0:T(8,128)(2,1)}, bf16[256,2048]{1,0:T(8,128)(2,1)}, u32[]{:S(2)}, u32[]{:S(2)}) %collective-permute-start.38) | collective-permute-done | bytes 1048608 | tf_op jit(solution)/shard_map/ppermute | solution.py:87
  416.3 2.0 copy.89
  421.7 2.3 fusion.62
  426.6 3.2 pad_maximum_fusion.1
  429.8 11.0 %rev.16 = f32[128,2,2048]{2,1,0:T(2,128)} reverse(f32[128,2,2048]{2,1,0:T(2,128)} %pad_maximum_fusion.1), dimensions={1} | reverse | bytes 4194304 | tf_op jit(solution)/shard_map/jit(_flip)/rev | solution.py:120
  440.8 3.4 broadcast_select_fusion.1
  444.2 3.0 copy.96
  448.7 3.2 pad_maximum_fusion.2
  451.9 11.0 %rev.17 = f32[128,2,2048]{2,1,0:T(2,128)} reverse(f32[128,2,2048]{2,1,0:T(2,128)} %pad_maximum_fusion.2), dimensions={1} | reverse | bytes 4194304 | tf_op jit(solution)/shard_map/jit(_flip)/rev | solution.py:120
  462.9 2.2 broadcast_select_fusion
  468.4 2.3 multiply_reduce_fusion
  473.4 6.2 %all-to-all-start.4 = ((bf16[8,128,384]{2,1,0:T(8,128)(2,1)}), bf16[8,128,384]{2,1,0:T(8,128)(2,1)}, u32[]{:S(2)}, u32[]{:S(2)}) async-start(bf16[8,128,384]{2,1,0:T(8,128)(2,1)} %fusion.62), calls=%async_computation.4 | async-start | bytes 1572864 | tf_op jit(solution)/shard_map/all_to_all | solution.py:109
  480.0 3.9 fusion.104
  489.6 12.1 %collective-permute-done.9 = bf16[128,2048]{1,0:T(8,128)(2,1)S(1)} collective-permute-done((bf16[128,2048]{1,0:T(8,128)(2,1)S(1)}, bf16[128,2048]{1,0:T(8,128)(2,1)S(1)}, u32[]{:S(2)}, u32[]{:S(2)}) %collective-permute-start.9) | collective-permute-done | bytes 524320 | tf_op jit(solution)/shard_map/ppermute | solution.py:99
  509.1 2.0 copy.77
  513.1 2.3 fusion.46
  (324 shorter events, 134.6 us)
Async XLA Ops:
  0.6 31.3 %collective-permute-start.5 = (bf16[128,2048]{1,0:T(8,128)(2,1)}, bf16[128,2048]{1,0:T(8,128)(2,1)S(1)}, u32[]{:S(2)}, u32[]{:S(2)}) collective-permute-start(bf16[128,2048]{1,0:T(8,128)(2,1)} %param.23), channel_id=1, source_target_pairs={{0,2},{2,0},{4,6},{6,4},{8,10},{10,8},{12,14},{14,12},{16,18},{18,... | collective-permute-start | bytes 1572872 | tf_op jit(solution)/shard_map/ppermute | solution.py:87
  1.2 25.4 %collective-permute-start.32 = (bf16[128,2048]{1,0:T(8,128)(2,1)}, bf16[128,2048]{1,0:T(8,128)(2,1)}, u32[]{:S(2)}, u32[]{:S(2)}) collective-permute-start(bf16[128,2048]{1,0:T(8,128)(2,1)} %param.23), channel_id=1, source_target_pairs={{0,8},{2,10},{4,12},{6,14},{8,16},{10,18},{12,20},{14,22},{16,24},... | collective-permute-start | bytes 1572872 | tf_op jit(solution)/shard_map/ppermute | solution.py:87
  7.1 91.6 %collective-permute-start.13 = (bf16[128,2048]{1,0:T(8,128)(2,1)S(1)}, bf16[128,2048]{1,0:T(8,128)(2,1)S(1)}, u32[]{:S(2)}, u32[]{:S(2)}) collective-permute-start(bf16[128,2048]{1,0:T(8,128)(2,1)S(1)} %get-tuple-element.36), channel_id=1, source_target_pairs={{0,4},{2,6},{4,0},{6,2},{8,12},{10,14},{12,8},{14,10},{16,20},{18,... | collective-permute-start | bytes 1572872 | tf_op jit(solution)/shard_map/ppermute | solution.py:87
  8.6 21.6 %collective-permute-start.10 = (bf16[128,2048]{1,0:T(8,128)(2,1)S(1)}, bf16[128,2048]{1,0:T(8,128)(2,1)}, u32[]{:S(2)}, u32[]{:S(2)}) collective-permute-start(bf16[128,2048]{1,0:T(8,128)(2,1)S(1)} %get-tuple-element.36), channel_id=1, source_target_pairs={{0,8},{2,10},{4,12},{6,14},{8,16},{10,18},{12,20},{14,22},{16,24},... | collective-permute-start | bytes 1572872 | tf_op jit(solution)/shard_map/ppermute | solution.py:87
  18.7 61.6 %all-to-all-start = ((bf16[8,128,384]{2,1,0:T(8,128)(2,1)}), bf16[8,128,384]{2,1,0:T(8,128)(2,1)S(1)}, u32[]{:S(2)}, u32[]{:S(2)}) async-start(bf16[8,128,384]{2,1,0:T(8,128)(2,1)} %bitcast.3), calls=%async_computation | async-start | bytes 1572864 | tf_op jit(solution)/shard_map/all_to_all | solution.py:109
  23.3 18.2 %copy-start.50 = (pred[8]{0:T(512)(128)(4,1)}, pred[8]{0:T(512)(128)(4,1)S(1)}, u32[]{:S(2)}) copy-start(pred[8]{0:T(512)(128)(4,1)S(1)} %compare_and_fusion) | copy-start | bytes 28
  26.6 57.0 %collective-permute-start.35 = (bf16[128,2048]{1,0:T(8,128)(2,1)}, bf16[128,2048]{1,0:T(8,128)(2,1)}, u32[]{:S(2)}, u32[]{:S(2)}) collective-permute-start(bf16[128,2048]{1,0:T(8,128)(2,1)} %collective-permute-done.32), channel_id=1, source_target_pairs={{0,2},{2,0},{4,6},{6,4},{8,10},{10,8},{12,14},{14,12},{16,18},{18,... | collective-permute-start | bytes 1572872 | tf_op jit(solution)/shard_map/ppermute | solution.py:87
  26.7 27.6 %collective-permute-start.33 = (bf16[128,2048]{1,0:T(8,128)(2,1)}, bf16[128,2048]{1,0:T(8,128)(2,1)}, u32[]{:S(2)}, u32[]{:S(2)}) collective-permute-start(bf16[128,2048]{1,0:T(8,128)(2,1)} %collective-permute-done.32), channel_id=1, source_target_pairs={{0,8},{2,10},{4,12},{6,14},{8,16},{10,18},{12,20},{14,22},{16,24},... | collective-permute-start | bytes 1572872 | tf_op jit(solution)/shard_map/ppermute | solution.py:87
  30.2 70.9 %collective-permute-start.14 = (bf16[128,2048]{1,0:T(8,128)(2,1)}, bf16[128,2048]{1,0:T(8,128)(2,1)}, u32[]{:S(2)}, u32[]{:S(2)}) collective-permute-start(bf16[128,2048]{1,0:T(8,128)(2,1)} %collective-permute-done.10), channel_id=1, source_target_pairs={{0,4},{2,6},{4,0},{6,2},{8,12},{10,14},{12,8},{14,10},{16,20},{18,... | collective-permute-start | bytes 1572872 | tf_op jit(solution)/shard_map/ppermute | solution.py:87
  31.9 33.5 %collective-permute-start.11 = (bf16[128,2048]{1,0:T(8,128)(2,1)}, bf16[128,2048]{1,0:T(8,128)(2,1)S(1)}, u32[]{:S(2)}, u32[]{:S(2)}) collective-permute-start(bf16[128,2048]{1,0:T(8,128)(2,1)} %collective-permute-done.10), channel_id=1, source_target_pairs={{0,8},{2,10},{4,12},{6,14},{8,16},{10,18},{12,20},{14,22},{16,24},... | collective-permute-start | bytes 1572872 | tf_op jit(solution)/shard_map/ppermute | solution.py:87
  43.4 39.3 %copy-start.36 = (bf16[128,2048]{1,0:T(8,128)(2,1)S(1)}, bf16[128,2048]{1,0:T(8,128)(2,1)}, u32[]{:S(2)}) copy-start(bf16[128,2048]{1,0:T(8,128)(2,1)} %copy-done.35) | copy-start | bytes 1572868
  54.3 26.2 %collective-permute-start.34 = (bf16[128,2048]{1,0:T(8,128)(2,1)}, bf16[128,2048]{1,0:T(8,128)(2,1)}, u32[]{:S(2)}, u32[]{:S(2)}) collective-permute-start(bf16[128,2048]{1,0:T(8,128)(2,1)} %collective-permute-done.33), channel_id=1, source_target_pairs={{0,8},{2,10},{4,12},{6,14},{8,16},{10,18},{12,20},{14,22},{16,24},... | collective-permute-start | bytes 1572872 | tf_op jit(solution)/shard_map/ppermute | solution.py:87
  65.4 21.6 %collective-permute-start.36 = (bf16[128,2048]{1,0:T(8,128)(2,1)}, bf16[128,2048]{1,0:T(8,128)(2,1)}, u32[]{:S(2)}, u32[]{:S(2)}) collective-permute-start(bf16[128,2048]{1,0:T(8,128)(2,1)} %collective-permute-done.33), channel_id=1, source_target_pairs={{0,2},{2,0},{4,6},{6,4},{8,10},{10,8},{12,14},{14,12},{16,18},{18,... | collective-permute-start | bytes 1572872 | tf_op jit(solution)/shard_map/ppermute | solution.py:87
  80.5 16.2 %collective-permute-start.12 = (bf16[128,2048]{1,0:T(8,128)(2,1)}, bf16[128,2048]{1,0:T(8,128)(2,1)}, u32[]{:S(2)}, u32[]{:S(2)}) collective-permute-start(bf16[128,2048]{1,0:T(8,128)(2,1)} %copy-done.39), channel_id=1, source_target_pairs={{0,8},{2,10},{4,12},{6,14},{8,16},{10,18},{12,20},{14,22},{16,24},... | collective-permute-start | bytes 1572872 | tf_op jit(solution)/shard_map/ppermute | solution.py:87
  83.6 29.9 %collective-permute-start.15 = (bf16[128,2048]{1,0:T(8,128)(2,1)}, bf16[128,2048]{1,0:T(8,128)(2,1)S(1)}, u32[]{:S(2)}, u32[]{:S(2)}) collective-permute-start(bf16[128,2048]{1,0:T(8,128)(2,1)} %copy-done.39), channel_id=1, source_target_pairs={{0,4},{2,6},{4,0},{6,2},{8,12},{10,14},{12,8},{14,10},{16,20},{18,... | collective-permute-start | bytes 1572872 | tf_op jit(solution)/shard_map/ppermute | solution.py:87
  87.0 15.9 %collective-permute-start = (bf16[8,1,128,256]{3,2,0,1:T(8,128)(2,1)S(1)}, bf16[8,1,128,256]{3,2,0,1:T(8,128)(2,1)S(1)}, u32[]{:S(2)}, u32[]{:S(2)}) collective-permute-start(bf16[8,1,128,256]{3,2,0,1:T(8,128)(2,1)S(1)} %get-tuple-element.55), channel_id=1, source_target_pairs={{0,2},{2,0},{4,6},{6,4},{8,10},{10,8},{12,14},{14,12},{16,18},{18,... | collective-permute-start | bytes 1572872 | tf_op jit(solution)/shard_map/ppermute | solution.py:87
  96.8 17.5 %collective-permute-start.37 = (bf16[128,2048]{1,0:T(8,128)(2,1)}, bf16[128,2048]{1,0:T(8,128)(2,1)}, u32[]{:S(2)}, u32[]{:S(2)}) collective-permute-start(bf16[128,2048]{1,0:T(8,128)(2,1)} %collective-permute-done.34), channel_id=1, source_target_pairs={{0,2},{2,0},{4,6},{6,4},{8,10},{10,8},{12,14},{14,12},{16,18},{18,... | collective-permute-start | bytes 1572872 | tf_op jit(solution)/shard_map/ppermute | solution.py:87
  98.7 43.8 %collective-permute-start.16 = (bf16[128,2048]{1,0:T(8,128)(2,1)}, bf16[128,2048]{1,0:T(8,128)(2,1)S(1)}, u32[]{:S(2)}, u32[]{:S(2)}) collective-permute-start(bf16[128,2048]{1,0:T(8,128)(2,1)} %collective-permute-done.12), channel_id=1, source_target_pairs={{0,4},{2,6},{4,0},{6,2},{8,12},{10,14},{12,8},{14,10},{16,20},{18,... | collective-permute-start | bytes 1572872 | tf_op jit(solution)/shard_map/ppermute | solution.py:87
  103.4 153.3 %copy-start.13 = (bf16[8,1,2,128,256]{4,3,2,0,1:T(8,128)(2,1)}, bf16[8,1,2,128,256]{4,3,2,0,1:T(8,128)(2,1)S(1)}, u32[]{:S(2)}) copy-start(bf16[8,1,2,128,256]{4,3,2,0,1:T(8,128)(2,1)S(1)} %copy.61) | copy-start | bytes 3145732
  110.0 12.9 %all-to-all-start.1 = ((bf16[8,128,128]{2,1,0:T(8,128)(2,1)}), bf16[8,128,128]{2,1,0:T(8,128)(2,1)S(1)}, u32[]{:S(2)}, u32[]{:S(2)}) async-start(bf16[8,128,128]{2,1,0:T(8,128)(2,1)} %bitcast.9), calls=%async_computation.1 | async-start | bytes 524288 | tf_op jit(solution)/shard_map/all_to_all | solution.py:109
  123.2 19.0 %collective-permute-start.18 = (bf16[128,1024]{0,1:T(8,128)(2,1)S(1)}, bf16[128,1024]{0,1:T(8,128)(2,1)S(1)}, u32[]{:S(2)}, u32[]{:S(2)}) collective-permute-start(bf16[128,1024]{0,1:T(8,128)(2,1)S(1)} %bitcast.215), channel_id=1, source_target_pairs={{0,8},{2,10},{4,12},{6,14},{8,16},{10,18},{12,20},{14,22},{16,24},... | collective-permute-start | bytes 786440 | tf_op jit(solution)/shard_map/ppermute | solution.py:87
  127.4 27.2 %collective-permute-start.1 = (bf16[128,2048]{1,0:T(8,128)(2,1)S(1)}, bf16[128,2048]{1,0:T(8,128)(2,1)S(1)}, u32[]{:S(2)}, u32[]{:S(2)}) collective-permute-start(bf16[128,2048]{1,0:T(8,128)(2,1)S(1)} %convolution_convert_fusion), channel_id=1, source_target_pairs={{0,1},{1,0},{2,3},{3,2},{4,5},{5,4},{6,7},{7,6},{8,9},{9,8},{10,11... | collective-permute-start | bytes 1572872 | tf_op jit(solution)/shard_map/ppermute | solution.py:99
  142.2 9.9 %collective-permute-start.19 = (bf16[128,1024]{0,1:T(8,128)(2,1)S(1)}, bf16[128,1024]{0,1:T(8,128)(2,1)}, u32[]{:S(2)}, u32[]{:S(2)}) collective-permute-start(bf16[128,1024]{0,1:T(8,128)(2,1)S(1)} %collective-permute-done.18), channel_id=1, source_target_pairs={{0,8},{2,10},{4,12},{6,14},{8,16},{10,18},{12,20},{14,22},{16,24},... | collective-permute-start | bytes 786440 | tf_op jit(solution)/shard_map/ppermute | solution.py:87
  149.8 12.6 %collective-permute-start.21 = (bf16[128,1024]{0,1:T(8,128)(2,1)S(1)}, bf16[128,1024]{0,1:T(8,128)(2,1)S(1)}, u32[]{:S(2)}, u32[]{:S(2)}) collective-permute-start(bf16[128,1024]{0,1:T(8,128)(2,1)S(1)} %bitcast.217), channel_id=1, source_target_pairs={{0,4},{2,6},{4,0},{6,2},{8,12},{10,14},{12,8},{14,10},{16,20},{18,... | collective-permute-start | bytes 786440 | tf_op jit(solution)/shard_map/ppermute | solution.py:87
  150.2 14.5 %collective-permute-start.22 = (bf16[128,1024]{0,1:T(8,128)(2,1)S(1)}, bf16[128,1024]{0,1:T(8,128)(2,1)S(1)}, u32[]{:S(2)}, u32[]{:S(2)}) collective-permute-start(bf16[128,1024]{0,1:T(8,128)(2,1)S(1)} %collective-permute-done.18), channel_id=1, source_target_pairs={{0,4},{2,6},{4,0},{6,2},{8,12},{10,14},{12,8},{14,10},{16,20},{18,... | collective-permute-start | bytes 786440 | tf_op jit(solution)/shard_map/ppermute | solution.py:87
  152.1 18.2 %collective-permute-start.23 = (bf16[128,1024]{0,1:T(8,128)(2,1)}, bf16[128,1024]{0,1:T(8,128)(2,1)S(1)}, u32[]{:S(2)}, u32[]{:S(2)}) collective-permute-start(bf16[128,1024]{0,1:T(8,128)(2,1)} %collective-permute-done.19), channel_id=1, source_target_pairs={{0,4},{2,6},{4,0},{6,2},{8,12},{10,14},{12,8},{14,10},{16,20},{18,... | collective-permute-start | bytes 786440 | tf_op jit(solution)/shard_map/ppermute | solution.py:87
  152.4 8.4 %collective-permute-start.20 = (bf16[128,1024]{0,1:T(8,128)(2,1)}, bf16[128,1024]{0,1:T(8,128)(2,1)S(1)}, u32[]{:S(2)}, u32[]{:S(2)}) collective-permute-start(bf16[128,1024]{0,1:T(8,128)(2,1)} %collective-permute-done.19), channel_id=1, source_target_pairs={{0,8},{2,10},{4,12},{6,14},{8,16},{10,18},{12,20},{14,22},{16,24},... | collective-permute-start | bytes 786440 | tf_op jit(solution)/shard_map/ppermute | solution.py:87
  155.3 15.1 %collective-permute-start.2 = (bf16[128,2048]{1,0:T(8,128)(2,1)S(1)}, bf16[128,2048]{1,0:T(8,128)(2,1)S(1)}, u32[]{:S(2)}, u32[]{:S(2)}) collective-permute-start(bf16[128,2048]{1,0:T(8,128)(2,1)S(1)} %get-tuple-element.34), channel_id=1, source_target_pairs={{0,2},{2,0},{4,6},{6,4},{8,10},{10,8},{12,14},{14,12},{16,18},{18,... | collective-permute-start | bytes 1572872 | tf_op jit(solution)/shard_map/ppermute | solution.py:87
  160.8 42.0 %collective-permute-start.26 = (bf16[128,2048]{1,0:T(8,128)(2,1)S(1)}, bf16[128,2048]{1,0:T(8,128)(2,1)}, u32[]{:S(2)}, u32[]{:S(2)}) collective-permute-start(bf16[128,2048]{1,0:T(8,128)(2,1)S(1)} %get-tuple-element.34), channel_id=1, source_target_pairs={{0,8},{2,10},{4,12},{6,14},{8,16},{10,18},{12,20},{14,22},{16,24},... | collective-permute-start | bytes 1572872 | tf_op jit(solution)/shard_map/ppermute | solution.py:87
  162.4 42.6 %collective-permute-start.24 = (bf16[128,1024]{0,1:T(8,128)(2,1)S(1)}, bf16[128,1024]{0,1:T(8,128)(2,1)S(1)}, u32[]{:S(2)}, u32[]{:S(2)}) collective-permute-start(bf16[128,1024]{0,1:T(8,128)(2,1)S(1)} %collective-permute-done.20), channel_id=1, source_target_pairs={{0,4},{2,6},{4,0},{6,2},{8,12},{10,14},{12,8},{14,10},{16,20},{18,... | collective-permute-start | bytes 786440 | tf_op jit(solution)/shard_map/ppermute | solution.py:87
  196.2 9.0 %collective-permute-start.6 = (bf16[128,2048]{1,0:T(8,128)(2,1)S(1)}, bf16[128,2048]{1,0:T(8,128)(2,1)S(1)}, u32[]{:S(2)}, u32[]{:S(2)}) collective-permute-start(bf16[128,2048]{1,0:T(8,128)(2,1)S(1)} %slice.169), channel_id=1, source_target_pairs={{0,2},{2,0},{4,6},{6,4},{8,10},{10,8},{12,14},{14,12},{16,18},{18,... | collective-permute-start | bytes 1572872 | tf_op jit(solution)/shard_map/ppermute | solution.py:87
  202.2 3.6 collective-permute-start.3
  202.8 39.9 %collective-permute-start.29 = (bf16[128,2048]{1,0:T(8,128)(2,1)}, bf16[128,2048]{1,0:T(8,128)(2,1)}, u32[]{:S(2)}, u32[]{:S(2)}) collective-permute-start(bf16[128,2048]{1,0:T(8,128)(2,1)} %collective-permute-done.26), channel_id=1, source_target_pairs={{0,2},{2,0},{4,6},{6,4},{8,10},{10,8},{12,14},{14,12},{16,18},{18,... | collective-permute-start | bytes 1572872 | tf_op jit(solution)/shard_map/ppermute | solution.py:87
  202.9 16.4 %collective-permute-start.27 = (bf16[128,2048]{1,0:T(8,128)(2,1)}, bf16[128,2048]{1,0:T(8,128)(2,1)}, u32[]{:S(2)}, u32[]{:S(2)}) collective-permute-start(bf16[128,2048]{1,0:T(8,128)(2,1)} %collective-permute-done.26), channel_id=1, source_target_pairs={{0,8},{2,10},{4,12},{6,14},{8,16},{10,18},{12,20},{14,22},{16,24},... | collective-permute-start | bytes 1572872 | tf_op jit(solution)/shard_map/ppermute | solution.py:87
  205.0 25.5 %copy-start.29 = (bf16[128,2048]{1,0:T(8,128)(2,1)S(1)}, bf16[128,2048]{1,0:T(8,128)(2,1)}, u32[]{:S(2)}) copy-start(bf16[128,2048]{1,0:T(8,128)(2,1)} %param.23) | copy-start | bytes 1572868
  205.1 27.5 %copy-start.45 = (bf16[1024,1024]{0,1:T(8,128)(2,1)}, bf16[1024,1024]{0,1:T(8,128)(2,1)S(1)}, u32[]{:S(2)}) copy-start(bf16[1024,1024]{0,1:T(8,128)(2,1)S(1)} %constant_dynamic-update-slice_fusion.8) | copy-start | bytes 6291460
  205.3 15.3 %collective-permute-start.7 = (bf16[128,2048]{1,0:T(8,128)(2,1)S(1)}, bf16[128,2048]{1,0:T(8,128)(2,1)S(1)}, u32[]{:S(2)}, u32[]{:S(2)}) collective-permute-start(bf16[128,2048]{1,0:T(8,128)(2,1)S(1)} %fusion.51), channel_id=1, source_target_pairs={{0,1},{1,0},{2,3},{3,2},{4,5},{5,4},{6,7},{7,6},{8,9},{9,8},{10,11... | collective-permute-start | bytes 1572872 | tf_op jit(solution)/shard_map/ppermute | solution.py:99
  206.0 24.6 %collective-permute-start.4 = (bf16[128,2048]{1,0:T(8,128)(2,1)S(1)}, bf16[128,2048]{1,0:T(8,128)(2,1)S(1)}, u32[]{:S(2)}, u32[]{:S(2)}) collective-permute-start(bf16[128,2048]{1,0:T(8,128)(2,1)S(1)} %fusion.52), channel_id=1, source_target_pairs={{0,1},{1,0},{2,3},{3,2},{4,5},{5,4},{6,7},{7,6},{8,9},{9,8},{10,11... | collective-permute-start | bytes 1572872 | tf_op jit(solution)/shard_map/ppermute | solution.py:99
  219.3 25.4 %collective-permute-start.30 = (bf16[128,2048]{1,0:T(8,128)(2,1)}, bf16[128,2048]{1,0:T(8,128)(2,1)}, u32[]{:S(2)}, u32[]{:S(2)}) collective-permute-start(bf16[128,2048]{1,0:T(8,128)(2,1)} %collective-permute-done.27), channel_id=1, source_target_pairs={{0,2},{2,0},{4,6},{6,4},{8,10},{10,8},{12,14},{14,12},{16,18},{18,... | collective-permute-start | bytes 1572872 | tf_op jit(solution)/shard_map/ppermute | solution.py:87
  219.3 20.7 %collective-permute-start.28 = (bf16[128,2048]{1,0:T(8,128)(2,1)}, bf16[128,2048]{1,0:T(8,128)(2,1)}, u32[]{:S(2)}, u32[]{:S(2)}) collective-permute-start(bf16[128,2048]{1,0:T(8,128)(2,1)} %collective-permute-done.27), channel_id=1, source_target_pairs={{0,8},{2,10},{4,12},{6,14},{8,16},{10,18},{12,20},{14,22},{16,24},... | collective-permute-start | bytes 1572872 | tf_op jit(solution)/shard_map/ppermute | solution.py:87
  234.9 12.8 %all-to-all-start.2 = ((bf16[8,128,128]{2,1,0:T(8,128)(2,1)}), bf16[8,128,128]{2,1,0:T(8,128)(2,1)S(1)}, u32[]{:S(2)}, u32[]{:S(2)}) async-start(bf16[8,128,128]{2,1,0:T(8,128)(2,1)} %bitcast.180), calls=%async_computation.2 | async-start | bytes 524288 | tf_op jit(solution)/shard_map/all_to_all | solution.py:109
  240.0 34.0 %collective-permute-start.31 = (bf16[128,2048]{1,0:T(8,128)(2,1)}, bf16[128,2048]{1,0:T(8,128)(2,1)}, u32[]{:S(2)}, u32[]{:S(2)}) collective-permute-start(bf16[128,2048]{1,0:T(8,128)(2,1)} %collective-permute-done.28), channel_id=1, source_target_pairs={{0,2},{2,0},{4,6},{6,4},{8,10},{10,8},{12,14},{14,12},{16,18},{18,... | collective-permute-start | bytes 1572872 | tf_op jit(solution)/shard_map/ppermute | solution.py:87
  247.7 88.3 %all-to-all-start.5 = ((bf16[8,128,256]{2,1,0:T(8,128)(2,1)}), bf16[8,128,256]{2,1,0:T(8,128)(2,1)}, u32[]{:S(2)}, u32[]{:S(2)}) async-start(bf16[8,128,256]{2,1,0:T(8,128)(2,1)} %bitcast.178), calls=%async_computation.5 | async-start | bytes 1048576 | tf_op jit(solution)/shard_map/all_to_all | solution.py:109
  272.2 69.9 %collective-permute-start.8 = (bf16[8,1,128,256]{2,0,3,1:T(8,128)(2,1)}, bf16[8,1,128,256]{2,0,3,1:T(8,128)(2,1)}, u32[]{:S(2)}, u32[]{:S(2)}) collective-permute-start(bf16[8,1,128,256]{2,0,3,1:T(8,128)(2,1)} %convert_bitcast_fusion.1), channel_id=1, source_target_pairs={{0,2},{2,0},{4,6},{6,4},{8,10},{10,8},{12,14},{14,12},{16,18},{18,... | collective-permute-start | bytes 1572872 | tf_op jit(solution)/shard_map/ppermute | solution.py:87
  272.5 16.0 %slice-start = ((s8[16777216]{0:T(1024)(128)(4,1)}), s8[4194304]{0:T(1024)(128)(4,1)S(1)}, s32[]{:S(2)}) async-start(s8[16777216]{0:T(1024)(128)(4,1)} %bitcast.237), calls=%async_computation.6 | async-start | bytes 8388608
  275.1 13.3 %slice-start.1 = ((s8[16777216]{0:T(1024)(128)(4,1)}), s8[4194304]{0:T(1024)(128)(4,1)S(1)}, s32[]{:S(2)}) async-start(s8[16777216]{0:T(1024)(128)(4,1)} %bitcast.237), calls=%async_computation.7 | async-start | bytes 8388608
  307.5 20.8 %copy-start.21 = (f32[2048,512]{0,1:T(8,128)}, f32[2048,512]{0,1:T(8,128)S(1)}, u32[]{:S(2)}) copy-start(f32[2048,512]{0,1:T(8,128)S(1)} %fusion.20) | copy-start | bytes 12582916
  319.4 13.5 %copy-start.23 = (f32[512,2048]{1,0:T(8,128)}, f32[512,2048]{1,0:T(8,128)S(1)}, u32[]{:S(2)}) copy-start(f32[512,2048]{1,0:T(8,128)S(1)} %fusion.21) | copy-start | bytes 12582916
  329.7 80.1 %collective-permute-start.42 = (bf16[2048,256]{0,1:T(8,128)(2,1)}, bf16[2048,256]{0,1:T(8,128)(2,1)}, u32[]{:S(2)}, u32[]{:S(2)}) collective-permute-start(bf16[2048,256]{0,1:T(8,128)(2,1)} %fusion.50), channel_id=1, source_target_pairs={{0,4},{2,6},{4,0},{6,2},{8,12},{10,14},{12,8},{14,10},{16,20},{18,... | collective-permute-start | bytes 3145736 | tf_op jit(solution)/shard_map/ppermute | solution.py:87
  332.8 79.6 %collective-permute-start.40 = (bf16[256,2048]{1,0:T(8,128)(2,1)}, bf16[256,2048]{1,0:T(8,128)(2,1)}, u32[]{:S(2)}, u32[]{:S(2)}) collective-permute-start(bf16[256,2048]{1,0:T(8,128)(2,1)} %fusion.49), channel_id=1, source_target_pairs={{0,4},{2,6},{4,0},{6,2},{8,12},{10,14},{12,8},{14,10},{16,20},{18,... | collective-permute-start | bytes 3145736 | tf_op jit(solution)/shard_map/ppermute | solution.py:87
  334.1 73.1 %collective-permute-start.38 = (bf16[256,2048]{1,0:T(8,128)(2,1)}, bf16[256,2048]{1,0:T(8,128)(2,1)}, u32[]{:S(2)}, u32[]{:S(2)}) collective-permute-start(bf16[256,2048]{1,0:T(8,128)(2,1)} %fusion.48), channel_id=1, source_target_pairs={{0,4},{2,6},{4,0},{6,2},{8,12},{10,14},{12,8},{14,10},{16,20},{18,... | collective-permute-start | bytes 3145736 | tf_op jit(solution)/shard_map/ppermute | solution.py:87
  342.1 17.4 %collective-permute-start.25 = (bf16[1024,1,128]{2,0,1:T(8,128)(2,1)}, bf16[1024,1,128]{2,0,1:T(8,128)(2,1)}, u32[]{:S(2)}, u32[]{:S(2)}) collective-permute-start(bf16[1024,1,128]{2,0,1:T(8,128)(2,1)} %dynamic-slice_convert_fusion.6), channel_id=1, source_target_pairs={{0,2},{2,0},{4,6},{6,4},{8,10},{10,8},{12,14},{14,12},{16,18},{18,... | collective-permute-start | bytes 786440 | tf_op jit(solution)/shard_map/ppermute | solution.py:87
  346.6 126.8 %all-to-all-start.3 = ((bf16[8,128,384]{2,1,0:T(8,128)(2,1)}), bf16[8,128,384]{2,1,0:T(8,128)(2,1)S(1)}, u32[]{:S(2)}, u32[]{:S(2)}) async-start(bf16[8,128,384]{2,1,0:T(8,128)(2,1)} %pad_maximum_fusion.6), calls=%async_computation.3 | async-start | bytes 1572864 | tf_op jit(solution)/shard_map/all_to_all | solution.py:109
  353.6 53.6 %copy-start.24 = (f32[512,2048]{1,0:T(8,128)S(1)}, f32[512,2048]{1,0:T(8,128)}, u32[]{:S(2)}) copy-start(f32[512,2048]{1,0:T(8,128)} %copy-done.23) | copy-start | bytes 12582916
  359.5 50.3 %copy-start.22 = (f32[2048,512]{0,1:T(8,128)S(1)}, f32[2048,512]{0,1:T(8,128)}, u32[]{:S(2)}) copy-start(f32[2048,512]{0,1:T(8,128)} %copy-done.21) | copy-start | bytes 12582916
  359.5 62.2 %collective-permute-start.17 = (bf16[8,1,128,384]{3,2,1,0:T(8,128)(2,1)}, bf16[8,1,128,384]{3,2,1,0:T(8,128)(2,1)}, u32[]{:S(2)}, u32[]{:S(2)}) collective-permute-start(bf16[8,1,128,384]{3,2,1,0:T(8,128)(2,1)} %dynamic-slice_convert_fusion.3), channel_id=1, source_target_pairs={{0,2},{2,0},{4,6},{6,4},{8,10},{10,8},{12,14},{14,12},{16,18},{18,... | collective-permute-start | bytes 2359304 | tf_op jit(solution)/shard_map/ppermute | solution.py:87
  409.7 14.3 %collective-permute-start.39 = (bf16[128,2048]{1,0:T(8,128)(2,1)}, bf16[128,2048]{1,0:T(8,128)(2,1)}, u32[]{:S(2)}, u32[]{:S(2)}) collective-permute-start(bf16[128,2048]{1,0:T(8,128)(2,1)} %fusion.63), channel_id=1, source_target_pairs={{0,2},{2,0},{4,6},{6,4},{8,10},{10,8},{12,14},{14,12},{16,18},{18,... | collective-permute-start | bytes 1572872 | tf_op jit(solution)/shard_map/ppermute | solution.py:87
  418.4 52.4 %collective-permute-start.43 = (bf16[2048,128]{1,0:T(8,128)(2,1)}, bf16[2048,128]{1,0:T(8,128)(2,1)}, u32[]{:S(2)}, u32[]{:S(2)}) collective-permute-start(bf16[2048,128]{1,0:T(8,128)(2,1)} %bitcast.148), channel_id=1, source_target_pairs={{0,2},{2,0},{4,6},{6,4},{8,10},{10,8},{12,14},{14,12},{16,18},{18,... | collective-permute-start | bytes 1572872 | tf_op jit(solution)/shard_map/ppermute | solution.py:87
  419.6 27.6 %collective-permute-start.41 = (bf16[128,2048]{1,0:T(8,128)(2,1)}, bf16[128,2048]{1,0:T(8,128)(2,1)}, u32[]{:S(2)}, u32[]{:S(2)}) collective-permute-start(bf16[128,2048]{1,0:T(8,128)(2,1)} %fusion.64), channel_id=1, source_target_pairs={{0,2},{2,0},{4,6},{6,4},{8,10},{10,8},{12,14},{14,12},{16,18},{18,... | collective-permute-start | bytes 1572872 | tf_op jit(solution)/shard_map/ppermute | solution.py:87
  473.4 29.2 %all-to-all-start.4 = ((bf16[8,128,384]{2,1,0:T(8,128)(2,1)}), bf16[8,128,384]{2,1,0:T(8,128)(2,1)}, u32[]{:S(2)}, u32[]{:S(2)}) async-start(bf16[8,128,384]{2,1,0:T(8,128)(2,1)} %fusion.62), calls=%async_computation.4 | async-start | bytes 1572864 | tf_op jit(solution)/shard_map/all_to_all | solution.py:109
  486.1 15.7 %copy-start.41 = (f32[2048]{0:T(1024)S(1)}, f32[2048]{0:T(1024)}, u32[]{:S(2)}) copy-start(f32[2048]{0:T(1024)} %param.21) | copy-start | bytes 24580
  486.1 15.7 %copy-start.47 = (f32[128]{0:T(128)S(1)}, f32[128]{0:T(128)}, u32[]{:S(2)}) copy-start(f32[128]{0:T(128)} %copy-done.46) | copy-start | bytes 1540
  487.6 14.1 %collective-permute-start.9 = (bf16[128,2048]{1,0:T(8,128)(2,1)S(1)}, bf16[128,2048]{1,0:T(8,128)(2,1)S(1)}, u32[]{:S(2)}, u32[]{:S(2)}) collective-permute-start(bf16[128,2048]{1,0:T(8,128)(2,1)S(1)} %fusion.25), channel_id=1, source_target_pairs={{0,1},{1,0},{2,3},{3,2},{4,5},{5,4},{6,7},{7,6},{8,9},{9,8},{10,11... | collective-permute-start | bytes 1572872 | tf_op jit(solution)/shard_map/ppermute | solution.py:99
  512.5 3.6 collective-permute-start.44
  (44 other events, 269.8 us)
